TPU v7x, 32 devices: a whole 2x2x4 slice. The times are simulated.
32 devices in a mesh: groups: 2 (over y), patch: 16 (over z, x, core).
Axes of the slice: x: 2, y: 2, z: 4, core: 2. Of those that a mesh axis runs over, the one named last changes fastest.
Arguments:
- coarse_depth: float32 [32, 128, 128], P(('groups', 'patch')), parts along dimension 0, may hold values from 1 to 3
- coarse_momentum: float32 [2, 32, 128, 128], P(None, ('groups', 'patch')), parts along dimension 1, may hold values from -3 to 3
- coarse_bed: float32 [32, 128, 128], P(('groups', 'patch')), parts along dimension 0, may hold values from -0.1 to 0.1
- fine_depth: float32 [128, 128, 128], P(('groups', 'patch')), parts along dimension 0, may hold values from 1 to 3
- fine_momentum: float32 [2, 128, 128, 128], P(None, ('groups', 'patch')), parts along dimension 1, may hold values from -3 to 3
- fine_bed: float32 [128, 128, 128], P(('groups', 'patch')), parts along dimension 0, may hold values from -0.1 to 0.1
- coarse_neighbors: int32 [32, 4], P(('groups', 'patch')), parts along dimension 0, may hold values from -1 to 15, as said below
- coarse_children: int32 [32, 4], P(('groups', 'patch')), parts along dimension 0, may hold values from 0 to 63, as said below
- coarse_refined: int32 [32, 4], P(('groups', 'patch')), parts along dimension 0, may hold values from 0 to 1
- fine_parent: int32 [128], P(('groups', 'patch')), parts along dimension 0, may hold values from 0 to 15, as said below
- fine_block: int32 [128], P(('groups', 'patch')), parts along dimension 0, may hold values from 0 to 3, as said below
- fine_active: int32 [128], P(('groups', 'patch')), parts along dimension 0, may hold values from 0 to 1, as said below
- fine_neighbors: int32 [128, 4], P(('groups', 'patch')), parts along dimension 0, may hold values from -1 to 63, as said below
- fill_mode: int32 [128, 4], P(('groups', 'patch')), parts along dimension 0, may hold values from 0 to 1
Outputs:
- coarse_depth_out: float32 [32, 128, 128], P(('groups', 'patch')), parts along dimension 0
- coarse_momentum_out: float32 [2, 32, 128, 128], P(None, ('groups', 'patch')), parts along dimension 1
- fine_depth_out: float32 [128, 128, 128], P(('groups', 'patch')), parts along dimension 0
- fine_momentum_out: float32 [2, 128, 128, 128], P(None, ('groups', 'patch')), parts along dimension 1
There are 2 independent parts, one for each index of `groups`. A program takes and returns all parts, laid end to end along the dimension named above; each array names one. Nothing has to cross between parts.
Inputs may be any that keep to these rules, and one draw needn't show every extreme that they name: `coarse_neighbors`: coarse neighbours are symmetric and lie on a grid of 8 patches a row; patch numbers follow the grid row by row, rows alternating in direction, so two neighbours' numbers differ by at most 15. `fine_parent`: each fine slot's parent is held by the slot's device or the next one along the axis (the last device's next is the first). `fine_block`: each pair of parent and block belongs to exactly one slot. `fine_active`: equals coarse_refined of the slot's parent and block. `coarse_children`: each named child slot is held by the coarse patch's device or the one before it along the axis (the first device's one before is the last), and has that parent and block. `fine_neighbors`: A named neighbour is an active sibling of the same parent, held by the slot's device or one beside it, cyclically; symmetric.
All inputs are finite; a program needn't handle non-finite values.
Results may differ from a plain program's by a relative error of at most 0.0003.
Values sent between devices are 32-bit elements; how exact they have to be, the bound alone decides.
A program may use at most 128 MiB of HBM per device.

v0:
```python
import jax
import jax.numpy as jnp
import numpy as np
from jax import lax
from jax.sharding import PartitionSpec as P

STEPS = 2


GRAVITY = 9.81
CFL_NUMBER = 0.3
WALL_SIGN = np.array(
    [[1.0, -1.0, 1.0, 1.0], [1.0, -1.0, 1.0, 1.0], [1.0, 1.0, -1.0, 1.0], [1.0, 1.0, -1.0, 1.0]],
    np.float32,
)
SUB_OFFSETS = np.array([-0.375, -0.125, 0.125, 0.375], np.float32)


def passed_along(array, axis, by):
    devices = lax.axis_size(axis)
    return lax.ppermute(array, axis, [(i, (i + by) % devices) for i in range(devices)])


def padded_2(array, sides, width):
    for axis, dim in sides:
        devices, length = (lax.axis_size(axis), array.shape[dim])
        up = [(i, (i + 1) % devices) for i in range(devices)]
        down = [(j, i) for i, j in up]
        last = lax.slice_in_dim(array, length - width, length, axis=dim)
        initial = lax.slice_in_dim(array, 0, width, axis=dim)
        before = lax.ppermute(last, axis, up)
        after = lax.ppermute(initial, axis, down)
        array = jnp.concatenate([before, array, after], axis=dim)
    return array


def rusanov(depth_left, normal_left, along_left, depth_right, normal_right, along_right):
    speed_left = normal_left / depth_left
    speed_right = normal_right / depth_right
    wave_speed = jnp.maximum(
        jnp.abs(speed_left) + jnp.sqrt(GRAVITY * depth_left),
        jnp.abs(speed_right) + jnp.sqrt(GRAVITY * depth_right),
    )
    flux_depth = 0.5 * (normal_left + normal_right) - 0.5 * wave_speed * (depth_right - depth_left)
    flux_normal = 0.5 * (
        normal_left * speed_left
        + normal_right * speed_right
        + 0.5 * GRAVITY * (depth_left * depth_left + depth_right * depth_right)
    ) - 0.5 * wave_speed * (normal_right - normal_left)
    flux_along = 0.5 * (along_left * speed_left + along_right * speed_right) - 0.5 * wave_speed * (
        along_right - along_left
    )
    return (flux_depth, flux_normal, flux_along)


def advance(padded, step_ratio):
    row_depth = padded[0, :, 1:-1, :]
    row_east = padded[1, :, 1:-1, :]
    row_north = padded[2, :, 1:-1, :]
    xflux_depth, xflux_east, xflux_north = rusanov(
        row_depth[:, :, :-1],
        row_east[:, :, :-1],
        row_north[:, :, :-1],
        row_depth[:, :, 1:],
        row_east[:, :, 1:],
        row_north[:, :, 1:],
    )
    col_depth = padded[0, :, :, 1:-1]
    col_east = padded[1, :, :, 1:-1]
    col_north = padded[2, :, :, 1:-1]
    yflux_depth, yflux_north, yflux_east = rusanov(
        col_depth[:, :-1],
        col_north[:, :-1],
        col_east[:, :-1],
        col_depth[:, 1:],
        col_north[:, 1:],
        col_east[:, 1:],
    )
    centre = padded[:, :, 1:-1, 1:-1]
    bed_level = padded[3]
    slope_east = 0.5 * (bed_level[:, 1:-1, 2:] - bed_level[:, 1:-1, :-2])
    slope_north = 0.5 * (bed_level[:, 2:, 1:-1] - bed_level[:, :-2, 1:-1])
    new_depth = centre[0] - step_ratio * (
        xflux_depth[:, :, 1:] - xflux_depth[:, :, :-1] + yflux_depth[:, 1:] - yflux_depth[:, :-1]
    )
    new_east = centre[1] - step_ratio * (
        xflux_east[:, :, 1:]
        - xflux_east[:, :, :-1]
        + yflux_east[:, 1:]
        - yflux_east[:, :-1]
        + GRAVITY * centre[0] * slope_east
    )
    new_north = centre[2] - step_ratio * (
        xflux_north[:, :, 1:]
        - xflux_north[:, :, :-1]
        + yflux_north[:, 1:]
        - yflux_north[:, :-1]
        + GRAVITY * centre[0] * slope_north
    )
    return jnp.stack([new_depth, new_east, new_north, centre[3]])


def with_ghosts(state, ghosts):
    west_side = jnp.transpose(ghosts[:, 0], (1, 0, 2))
    east_side = jnp.transpose(ghosts[:, 1], (1, 0, 2))
    south_side = jnp.transpose(ghosts[:, 2], (1, 0, 2))
    north_side = jnp.transpose(ghosts[:, 3], (1, 0, 2))
    middle = jnp.concatenate([west_side[..., None], state, east_side[..., None]], axis=3)
    corner = jnp.zeros_like(west_side[..., :1])
    bottom = jnp.concatenate([corner, south_side, corner], axis=2)[:, :, None, :]
    summit = jnp.concatenate([corner, north_side, corner], axis=2)[:, :, None, :]
    return jnp.concatenate([bottom, middle, summit], axis=2)


def edge_strips(state):
    sides = jnp.stack(
        [state[:, :, :, 0], state[:, :, :, -1], state[:, :, 0, :], state[:, :, -1, :]]
    )
    return jnp.transpose(sides, (2, 0, 1, 3))


def opposite_strips(table, index):
    found = jnp.take(table, index, axis=0)
    return jnp.stack([found[:, 0, 1], found[:, 1, 0], found[:, 2, 3], found[:, 3, 2]], axis=1)


def cycle_lines(state, quarter):
    line_pos = [quarter - 1, 2 * quarter - 1, 2 * quarter, 3 * quarter]
    columns = [state[:, :, :, place] for place in line_pos]
    rowlines = [state[:, :, place, :] for place in line_pos]
    return jnp.transpose(jnp.stack(columns + rowlines), (2, 1, 0, 3))


def coarse_fill(face_lines, block_ids, mode_ids, quarter):
    col_block = 1 + block_ids % 2
    row_block = 1 + block_ids // 2
    line_index = jnp.stack([col_block - 1, col_block + 1, 3 + row_block, 5 + row_block], axis=1)
    start_cell = quarter * jnp.stack([row_block, row_block, col_block, col_block], axis=1)
    pick_table = (line_index[:, :, None] == jnp.arange(8)[None, None, :]).astype(jnp.float32)
    chosen = jnp.einsum("psl,pcln->pscn", pick_table, face_lines, precision=lax.Precision.HIGHEST)
    positions = start_cell[:, :, None] - 1 + jnp.arange(quarter + 2)[None, None, :]
    positions = jnp.broadcast_to(positions[:, :, None, :], chosen.shape[:3] + (quarter + 2,))
    window = jnp.take_along_axis(chosen, positions, axis=3)
    middle_val = window[..., 1:-1]
    rising = window[..., 2:] - middle_val
    falling = middle_val - window[..., :-2]
    slope_val = jnp.where(
        rising * falling > 0, jnp.sign(rising) * jnp.minimum(jnp.abs(rising), jnp.abs(falling)), 0.0
    )
    weight_mode = mode_ids.astype(jnp.float32)[:, :, None, None]
    return jnp.repeat(middle_val, 4, axis=3) + weight_mode * jnp.repeat(
        slope_val, 4, axis=3
    ) * jnp.tile(jnp.asarray(SUB_OFFSETS), quarter)


def top_speed(state, live):
    depth_now = state[0]
    fastest = jnp.maximum(jnp.abs(state[1] / depth_now), jnp.abs(state[2] / depth_now)) + jnp.sqrt(
        GRAVITY * depth_now
    )
    return jnp.max(fastest * live[:, None, None])


def restrict_blocks(state, quarter):
    part_state = state[:3]
    patch_count = state.shape[1]
    blocks = part_state.reshape(3, patch_count, quarter, 4, quarter, 4).mean(axis=(3, 5))
    return jnp.transpose(blocks, (1, 0, 2, 3))


def insert_blocks(coarse, blocks, refined, quarter):
    for block_id in range(4):
        row_start = quarter * (1 + block_id // 2)
        col_start = quarter * (1 + block_id % 2)
        region = coarse[:3, :, row_start : row_start + quarter, col_start : col_start + quarter]
        fresh = jnp.transpose(blocks[:, block_id], (1, 0, 2, 3))
        merged = jnp.where(refined[:, block_id][None, :, None, None] > 0, fresh, region)
        coarse = coarse.at[
            :3, :, row_start : row_start + quarter, col_start : col_start + quarter
        ].set(merged)
    return coarse


def local(
    coarse_depth,
    coarse_momentum,
    coarse_bed,
    fine_depth,
    fine_momentum,
    fine_bed,
    coarse_neighbors,
    coarse_children,
    coarse_refined,
    fine_parent,
    fine_block,
    fine_active,
    fine_neighbors,
    fill_mode,
):
    quarter = coarse_depth.shape[-1] // 4
    patch_count = coarse_depth.shape[0]
    slot_count = fine_depth.shape[0]
    device_count = lax.axis_size("patch")
    device_index = lax.axis_index("patch")
    fine_total = slot_count * device_count
    coarse_total = patch_count * device_count
    coarse = jnp.concatenate([coarse_depth[None], coarse_momentum, coarse_bed[None]])
    fine = jnp.concatenate([fine_depth[None], fine_momentum, fine_bed[None]])
    live = fine_active.astype(jnp.float32)
    every_coarse = jnp.ones((patch_count,), jnp.float32)
    coarse_valid = (coarse_neighbors >= 0)[:, :, None, None]
    fine_valid = (fine_neighbors >= 0)[:, :, None, None]
    sibling_index = jnp.mod(fine_neighbors - device_index * slot_count + slot_count, fine_total)
    parent_index = jnp.mod(fine_parent - device_index * patch_count, coarse_total)
    child_index = jnp.mod(coarse_children - device_index * slot_count + slot_count, fine_total)
    for coarse_step in range(STEPS):
        local_fast = jnp.maximum(top_speed(coarse, every_coarse), top_speed(fine, live))
        fastest_all = lax.pmax(local_fast, "patch")
        step_ratio = CFL_NUMBER / fastest_all
        strips = edge_strips(coarse)
        wall_ghosts = strips * jnp.asarray(WALL_SIGN)[None, :, :, None]
        strip_table = lax.all_gather(strips, "patch", axis=0, tiled=True)
        found_ghosts = opposite_strips(strip_table, jnp.maximum(coarse_neighbors, 0))
        ghosts = jnp.where(coarse_valid, found_ghosts, wall_ghosts)
        advanced = advance(with_ghosts(coarse, ghosts), step_ratio)
        both_states = jnp.stack(
            [jnp.transpose(coarse, (1, 0, 2, 3)), jnp.transpose(advanced, (1, 0, 2, 3))], axis=1
        )
        next_states = passed_along(both_states, "patch", -1)
        near_states = jnp.concatenate([both_states, next_states], axis=0)
        near_lines = jnp.stack(
            [
                cycle_lines(jnp.transpose(near_states[:, 0], (1, 0, 2, 3)), quarter),
                cycle_lines(jnp.transpose(near_states[:, 1], (1, 0, 2, 3)), quarter),
            ],
            axis=1,
        )
        picked = jnp.take(near_lines, parent_index, axis=0)
        old_lines = picked[:, 0]
        new_lines = picked[:, 1]
        for substep in range(4):
            weight_new = substep / 4.0
            face_lines = (1.0 - weight_new) * old_lines + weight_new * new_lines
            from_coarse = coarse_fill(face_lines, fine_block, fill_mode, quarter)
            fine_strips = edge_strips(fine)
            near_strips = padded_2(fine_strips, (("patch", 0),), slot_count)
            ghosts_fine = jnp.where(
                fine_valid, opposite_strips(near_strips, sibling_index), from_coarse
            )
            stepped = advance(with_ghosts(fine, ghosts_fine), step_ratio)
            fine = jnp.where(live[None, :, None, None] > 0, stepped, fine)
        block_means = restrict_blocks(fine, quarter).reshape(slot_count, -1)
        prior_means = passed_along(block_means, "patch", 1)
        near_means = jnp.concatenate([prior_means, block_means], axis=0)
        blocks = jnp.take(near_means, child_index, axis=0).reshape(
            patch_count, 4, 3, quarter, quarter
        )
        coarse = insert_blocks(advanced, blocks, coarse_refined, quarter)
    return (coarse[0], coarse[1:3], fine[0], fine[1:3])


def solution(mesh):
    return jax.shard_map(
        local,
        mesh=mesh,
        in_specs=(
            P(("groups", "patch"), None, None),
            P(None, ("groups", "patch"), None, None),
            P(("groups", "patch"), None, None),
            P(("groups", "patch"), None, None),
            P(None, ("groups", "patch"), None, None),
            P(("groups", "patch"), None, None),
            P(("groups", "patch"), None),
            P(("groups", "patch"), None),
            P(("groups", "patch"), None),
            P(("groups", "patch")),
            P(("groups", "patch")),
            P(("groups", "patch")),
            P(("groups", "patch"), None),
            P(("groups", "patch"), None),
        ),
        out_specs=(
            P(("groups", "patch"), None, None),
            P(None, ("groups", "patch"), None, None),
            P(("groups", "patch"), None, None),
            P(None, ("groups", "patch"), None, None),
        ),
        check_vma=False,
    )
```

profile of v0, /device:TPU:1, one launch (start us, length us, event | category | flops | bytes accessed | tf_op | source)
XLA Modules:
  0.0 718.7 jit_solution(17223768056344579060)
XLA Ops:
  10.7 21.2 %all-gather = f32[64,4,1,128]{3,1,2,0:T(4,128)S(1)} all-gather(f32[4,4,1,128]{3,1,2,0:T(4,128)S(1)} %fusion.255), channel_id=2, replica_groups=mesh['groups'=2,'patch'=16] {'patch'}, dimensions={0}, use_global_device_ids=true | all-gather | bytes 139264 | tf_op jit(solution)/shard_map/all_gather | solution.py:222
  35.3 29.5 %pmax.14 = f32[]{:T(128)} all-reduce(f32[]{:T(128)S(6)} %max.96), channel_id=1, replica_groups=mesh['groups'=2,'patch'=16] {'patch'}, use_global_device_ids=true, to_apply=%region_2.3 | all-reduce | flops 1 | bytes 8 | tf_op jit(solution)/shard_map/pmax | solution.py:218
  96.2 21.6 %gather_fusion.9 = f32[2176]{0:T(1024)S(1)} fusion(f32[4,4,4,128]{3,1,2,0:T(4,128)S(1)} %fusion.189, s32[2176]{0:T(1024)S(1)} %reshape.1034), kind=kCustom, calls=%fused_computation.16.clone | custom fusion | bytes 52224 | tf_op jit(solution)/shard_map/jit(take_along_axis)/gather | solution.py:143
  118.1 21.6 %gather_fusion.7 = f32[2176]{0:T(1024)S(1)} fusion(f32[4,4,4,128]{3,1,2,0:T(4,128)S(1)} %fusion.193, s32[2176]{0:T(1024)S(1)} %reshape.1034), kind=kCustom, calls=%fused_computation.15.clone | custom fusion | bytes 52224 | tf_op jit(solution)/shard_map/jit(take_along_axis)/gather | solution.py:143
  139.9 21.6 %gather_fusion.5 = f32[2176]{0:T(1024)S(1)} fusion(f32[4,4,4,128]{3,1,2,0:T(4,128)S(1)} %fusion.196, s32[2176]{0:T(1024)S(1)} %reshape.1034), kind=kCustom, calls=%fused_computation.14.clone | custom fusion | bytes 52224 | tf_op jit(solution)/shard_map/jit(take_along_axis)/gather | solution.py:143
  161.7 22.1 %gather_fusion.3 = f32[2176]{0:T(1024)S(1)} fusion(f32[4,4,4,128]{3,1,2,0:T(4,128)S(1)} %fusion.200, s32[2176]{0:T(1024)S(1)} %reshape.1034), kind=kCustom, calls=%fused_computation.3.clone | custom fusion | bytes 52224 | tf_op jit(solution)/shard_map/jit(take_along_axis)/gather | solution.py:143
  272.9 28.5 %reshape.775 = f32[3,4,32,4,32,4]{5,4,3,2,1,0:T(8,128)} reshape(f32[3,4,128,128]{3,2,1,0:T(8,128)} %copy.1006) | data formatting | bytes 1572864 | tf_op jit(solution)/shard_map/reshape | solution.py:167
  301.3 10.1 %reduce_sum.18 = f32[3,4,32,32]{3,2,1,0:T(8,128)} reduce(f32[3,4,32,4,32,4]{5,4,3,2,1,0:T(8,128)} %reshape.775, f32[]{:T(128)} %constant.408.clone.1), dimensions={3,5}, to_apply=%region_3.8 | reduce | flops 184320 | bytes 835588 | tf_op jit(solution)/shard_map/reduce_sum | solution.py:167
  327.5 9.8 %scatter.26 = f32[4,1,128,128]{3,0,2,1:T(4,128)S(1)} dynamic-update-slice(f32[4,1,128,128]{3,0,2,1:T(4,128)S(1)} %get-tuple-element.347, f32[3,1,32,32]{3,0,2,1:T(4,128)S(1)} %copy.1008, s32[]{:T(128)} %constant.406.clone.1, s32[]{:T(128)} %constant.406.clone.1, s32[]{:T(128)} %constant.421.clone.1, s32[]{:T(128)} %constant.421.clone.1) | dynamic-update-slice | bytes 24580 | tf_op jit(solution)/shard_map/scatter | solution.py:180
  340.0 11.7 %scatter.29 = f32[4,1,128,128]{3,0,2,1:T(4,128)S(1)} dynamic-update-slice(f32[4,1,128,128]{3,0,2,1:T(4,128)S(1)} %scatter.26, f32[3,1,32,32]{3,0,2,1:T(4,128)S(1)} %fusion.158, s32[]{:T(128)} %bitcast.249, s32[]{:T(128)} %constant.406.clone.1, s32[]{:T(128)} %bitcast.250, s32[]{:T(128)} %bitcast.251) | dynamic-update-slice | bytes 24580 | tf_op jit(solution)/shard_map/scatter | solution.py:180
  351.8 9.8 %scatter.30 = f32[4,1,128,128]{3,0,2,1:T(4,128)S(1)} dynamic-update-slice(f32[4,1,128,128]{3,0,2,1:T(4,128)S(1)} %scatter.29, f32[3,1,32,32]{3,0,2,1:T(4,128)S(1)} %slice_select_fusion.4, s32[]{:T(128)} %constant.406.clone.1, s32[]{:T(128)} %constant.406.clone.1, s32[]{:T(128)} %constant.414.clone.1, s32[]{:T(128)} %constant.421.clone.1) | dynamic-update-slice | bytes 24580 | tf_op jit(solution)/shard_map/scatter | solution.py:180
  361.7 9.8 %scatter.31 = f32[4,1,128,128]{3,0,2,1:T(4,128)S(1)} dynamic-update-slice(f32[4,1,128,128]{3,0,2,1:T(4,128)S(1)} %scatter.30, f32[3,1,32,32]{3,0,2,1:T(4,128)S(1)} %slice_select_fusion.3, s32[]{:T(128)} %constant.406.clone.1, s32[]{:T(128)} %constant.406.clone.1, s32[]{:T(128)} %constant.414.clone.1, s32[]{:T(128)} %constant.414.clone.1) | dynamic-update-slice | bytes 24580 | tf_op jit(solution)/shard_map/scatter | solution.py:180
  372.0 22.4 %all-gather.1 = f32[64,4,1,128]{3,1,2,0:T(4,128)S(1)} all-gather(f32[4,4,1,128]{3,1,2,0:T(4,128)S(1)} %fusion.254), channel_id=3, replica_groups=mesh['groups'=2,'patch'=16] {'patch'}, dimensions={0}, use_global_device_ids=true | all-gather | bytes 139264 | tf_op jit(solution)/shard_map/all_gather | solution.py:222
  400.2 29.7 %pmax.15 = f32[]{:T(128)} all-reduce(f32[]{:T(128)S(6)} %max.110), channel_id=1, replica_groups=mesh['groups'=2,'patch'=16] {'patch'}, use_global_device_ids=true, to_apply=%region_7.13 | all-reduce | flops 1 | bytes 8 | tf_op jit(solution)/shard_map/pmax | solution.py:218
  460.4 21.6 %gather_fusion.20 = f32[2176]{0:T(1024)S(1)} fusion(f32[4,4,4,128]{3,1,2,0:T(4,128)S(1)} %fusion.175, s32[2176]{0:T(1024)S(1)} %reshape.1034), kind=kCustom, calls=%fused_computation.20.clone | custom fusion | bytes 52224 | tf_op jit(solution)/shard_map/jit(take_along_axis)/gather | solution.py:143
  482.2 21.6 %gather_fusion.18 = f32[2176]{0:T(1024)S(1)} fusion(f32[4,4,4,128]{3,1,2,0:T(4,128)S(1)} %fusion.179, s32[2176]{0:T(1024)S(1)} %reshape.1034), kind=kCustom, calls=%fused_computation.19.clone | custom fusion | bytes 52224 | tf_op jit(solution)/shard_map/jit(take_along_axis)/gather | solution.py:143
  504.0 21.6 %gather_fusion.16 = f32[2176]{0:T(1024)S(1)} fusion(f32[4,4,4,128]{3,1,2,0:T(4,128)S(1)} %fusion.182, s32[2176]{0:T(1024)S(1)} %reshape.1034), kind=kCustom, calls=%fused_computation.18.clone | custom fusion | bytes 52224 | tf_op jit(solution)/shard_map/jit(take_along_axis)/gather | solution.py:143
  525.8 21.8 %gather_fusion.14 = f32[2176]{0:T(1024)S(1)} fusion(f32[4,4,4,128]{3,1,2,0:T(4,128)S(1)} %fusion.186, s32[2176]{0:T(1024)S(1)} %reshape.1034), kind=kCustom, calls=%fused_computation.17.clone | custom fusion | bytes 52224 | tf_op jit(solution)/shard_map/jit(take_along_axis)/gather | solution.py:143
  629.5 27.5 %reshape.789 = f32[3,4,32,4,32,4]{5,4,3,2,1,0:T(8,128)} reshape(f32[3,4,128,128]{3,2,1,0:T(8,128)S(1)} %copy.1117) | data formatting | bytes 1572864 | tf_op jit(solution)/shard_map/reshape | solution.py:167
  657.1 9.4 %reduce_sum.19 = f32[3,4,32,32]{3,2,1,0:T(8,128)S(1)} reduce(f32[3,4,32,4,32,4]{5,4,3,2,1,0:T(8,128)} %reshape.789, f32[]{:T(128)} %constant.408.clone.1), dimensions={3,5}, to_apply=%region_8.14 | reduce | flops 184320 | bytes 835588 | tf_op jit(solution)/shard_map/reduce_sum | solution.py:167
  672.8 9.8 %scatter.34 = f32[4,1,128,128]{3,0,2,1:T(4,128)S(1)} dynamic-update-slice(f32[4,1,128,128]{3,0,2,1:T(4,128)S(1)} %copy-done.22, f32[3,1,32,32]{3,0,2,1:T(4,128)S(1)} %fusion.145, s32[]{:T(128)} %constant.406.clone.1, s32[]{:T(128)} %constant.406.clone.1, s32[]{:T(128)} %constant.421.clone.1, s32[]{:T(128)} %constant.421.clone.1) | dynamic-update-slice | bytes 24580 | tf_op jit(solution)/shard_map/scatter | solution.py:180
  685.3 11.7 %scatter.35 = f32[4,1,128,128]{3,0,2,1:T(4,128)S(1)} dynamic-update-slice(f32[4,1,128,128]{3,0,2,1:T(4,128)S(1)} %scatter.34, f32[3,1,32,32]{3,0,2,1:T(4,128)S(1)} %fusion.144, s32[]{:T(128)} %bitcast.249, s32[]{:T(128)} %constant.406.clone.1, s32[]{:T(128)} %bitcast.250, s32[]{:T(128)} %bitcast.251) | dynamic-update-slice | bytes 24580 | tf_op jit(solution)/shard_map/scatter | solution.py:180
  697.1 9.8 %scatter.36 = f32[4,1,128,128]{3,0,2,1:T(4,128)S(1)} dynamic-update-slice(f32[4,1,128,128]{3,0,2,1:T(4,128)S(1)} %scatter.35, f32[3,1,32,32]{3,0,2,1:T(4,128)S(1)} %slice_select_fusion.1, s32[]{:T(128)} %constant.406.clone.1, s32[]{:T(128)} %constant.406.clone.1, s32[]{:T(128)} %constant.414.clone.1, s32[]{:T(128)} %constant.421.clone.1) | dynamic-update-slice | bytes 24580 | tf_op jit(solution)/shard_map/scatter | solution.py:180
  707.0 9.8 %scatter.39 = f32[4,1,128,128]{3,0,2,1:T(4,128)S(1)} dynamic-update-slice(f32[4,1,128,128]{3,0,2,1:T(4,128)S(1)} %scatter.36, f32[3,1,32,32]{3,0,2,1:T(4,128)S(1)} %slice_select_fusion, s32[]{:T(128)} %constant.406.clone.1, s32[]{:T(128)} %constant.406.clone.1, s32[]{:T(128)} %constant.414.clone.1, s32[]{:T(128)} %constant.414.clone.1) | dynamic-update-slice | bytes 24580 | tf_op jit(solution)/shard_map/scatter | solution.py:180
  (720 shorter events, 273.6 us)
Async XLA Ops:
  6.4 72.8 %collective-permute-start.1 = (f32[4,4,4,128]{3,2,1,0:T(4,128)S(1)}, f32[4,4,4,128]{3,2,1,0:T(4,128)}, u32[]{:S(2)}, u32[]{:S(2)}) collective-permute-start(f32[4,4,4,128]{3,2,1,0:T(4,128)S(1)} %maximum_bitcast_fusion.50), channel_id=1, source_target_pairs={{1,0},{2,1},{3,2},{4,3},{5,4},{6,5},{7,6},{8,7},{9,8},{10,9},{11,1... | collective-permute-start | bytes 98312 | tf_op jit(solution)/shard_map/ppermute | solution.py:32
  6.5 72.7 %collective-permute-start = (f32[4,4,4,128]{3,2,1,0:T(4,128)S(1)}, f32[4,4,4,128]{3,2,1,0:T(4,128)}, u32[]{:S(2)}, u32[]{:S(2)}) collective-permute-start(f32[4,4,4,128]{3,2,1,0:T(4,128)S(1)} %maximum_bitcast_fusion.50), channel_id=1, source_target_pairs={{0,1},{1,2},{2,3},{3,4},{4,5},{5,6},{6,7},{7,8},{8,9},{9,10},{10,1... | collective-permute-start | bytes 98312 | tf_op jit(solution)/shard_map/ppermute | solution.py:31
  67.7 13.1 %collective-permute-start.2 = (f32[1,2,4,128,128]{4,2,0,3,1:T(4,128)}, f32[1,2,4,128,128]{4,2,0,3,1:T(4,128)}, u32[]{:S(2)}, u32[]{:S(2)}) collective-permute-start(f32[1,2,4,128,128]{4,2,0,3,1:T(4,128)} %pad_maximum_fusion.58), channel_id=1, source_target_pairs={{0,15},{1,0},{2,1},{3,2},{4,3},{5,4},{6,5},{7,6},{8,7},{9,8},{10,9... | collective-permute-start | bytes 1572872 | tf_op jit(solution)/shard_map/ppermute | solution.py:21
  71.3 186.4 %copy-start.47 = (s32[1024]{0:T(1024)}, s32[1024]{0:T(1024)S(1)}, u32[]{:S(2)}) copy-start(s32[1024]{0:T(1024)S(1)} %pad_clamp_fusion.2) | copy-start | bytes 12292
  76.4 182.0 %copy-start.51 = (f32[128]{0:T(128)}, f32[128]{0:T(128)S(1)}, u32[]{:S(2)}) copy-start(f32[128]{0:T(128)S(1)} %mul.1608) | copy-start | bytes 1540
  76.7 110.0 %copy-start.61 = (pred[4,4]{0,1:T(4,128)(4,1)}, pred[4,4]{0,1:T(4,128)(4,1)S(1)}, u32[]{:S(2)}) copy-start(pred[4,4]{0,1:T(4,128)(4,1)S(1)} %copy.905) | copy-start | bytes 52
  188.5 71.8 %copy-start.30 = (f32[4,4,1]{2,1,0:T(4,128)}, f32[4,4,1]{2,1,0:T(4,128)S(1)}, u32[]{:S(2)}) copy-start(f32[4,4,1]{2,1,0:T(4,128)S(1)} %broadcast.461) | copy-start | bytes 196
  203.1 8.3 %collective-permute-start.4 = (f32[4,4,4,128]{3,2,0,1:T(4,128)}, f32[4,4,4,128]{3,2,0,1:T(4,128)}, u32[]{:S(2)}, u32[]{:S(2)}) collective-permute-start(f32[4,4,4,128]{3,2,0,1:T(4,128)} %maximum_bitcast_fusion.51), channel_id=1, source_target_pairs={{1,0},{2,1},{3,2},{4,3},{5,4},{6,5},{7,6},{8,7},{9,8},{10,9},{11,1... | collective-permute-start | bytes 98312 | tf_op jit(solution)/shard_map/ppermute | solution.py:32
  203.1 8.3 %collective-permute-start.3 = (f32[4,4,4,128]{3,2,0,1:T(4,128)}, f32[4,4,4,128]{3,2,0,1:T(4,128)}, u32[]{:S(2)}, u32[]{:S(2)}) collective-permute-start(f32[4,4,4,128]{3,2,0,1:T(4,128)} %maximum_bitcast_fusion.51), channel_id=1, source_target_pairs={{0,1},{1,2},{2,3},{3,4},{4,5},{5,6},{6,7},{7,8},{8,9},{9,10},{10,1... | collective-permute-start | bytes 98312 | tf_op jit(solution)/shard_map/ppermute | solution.py:31
  229.2 5.8 collective-permute-start.6
  229.3 5.7 collective-permute-start.5
  251.1 6.5 collective-permute-start.8
  254.5 3.1 collective-permute-start.7
  314.1 10.7 %collective-permute-start.9 = (f32[4,3072]{1,0:T(4,128)S(1)}, f32[4,3072]{1,0:T(4,128)}, u32[]{:S(2)}, u32[]{:S(2)}) collective-permute-start(f32[4,3072]{1,0:T(4,128)S(1)} %reshape.776), channel_id=1, source_target_pairs={{0,1},{1,2},{2,3},{3,4},{4,5},{5,6},{6,7},{7,8},{8,9},{9,10},{10,1... | collective-permute-start | bytes 147464 | tf_op jit(solution)/shard_map/ppermute | solution.py:21
  319.8 116.6 %collective-permute-start.11 = (f32[4,4,4,128]{3,2,0,1:T(4,128)}, f32[4,4,4,128]{3,2,0,1:T(4,128)}, u32[]{:S(2)}, u32[]{:S(2)}) collective-permute-start(f32[4,4,4,128]{3,2,0,1:T(4,128)} %maximum_bitcast_fusion.54), channel_id=1, source_target_pairs={{1,0},{2,1},{3,2},{4,3},{5,4},{6,5},{7,6},{8,7},{9,8},{10,9},{11,1... | collective-permute-start | bytes 98312 | tf_op jit(solution)/shard_map/ppermute | solution.py:32
  324.9 111.5 %collective-permute-start.10 = (f32[4,4,4,128]{3,2,0,1:T(4,128)}, f32[4,4,4,128]{3,2,0,1:T(4,128)}, u32[]{:S(2)}, u32[]{:S(2)}) collective-permute-start(f32[4,4,4,128]{3,2,0,1:T(4,128)} %maximum_bitcast_fusion.54), channel_id=1, source_target_pairs={{0,1},{1,2},{2,3},{3,4},{4,5},{5,6},{6,7},{7,8},{8,9},{9,10},{10,1... | collective-permute-start | bytes 98312 | tf_op jit(solution)/shard_map/ppermute | solution.py:31
  434.6 8.9 %collective-permute-start.12 = (f32[1,2,4,128,128]{4,2,3,1,0:T(4,128)}, f32[1,2,4,128,128]{4,2,3,1,0:T(4,128)}, u32[]{:S(2)}, u32[]{:S(2)}) collective-permute-start(f32[1,2,4,128,128]{4,2,3,1,0:T(4,128)} %pad_maximum_fusion.59), channel_id=1, source_target_pairs={{0,15},{1,0},{2,1},{3,2},{4,3},{5,4},{6,5},{7,6},{8,7},{9,8},{10,9... | collective-permute-start | bytes 1572872 | tf_op jit(solution)/shard_map/ppermute | solution.py:21
  563.7 7.1 collective-permute-start.14
  563.7 7.1 collective-permute-start.13
  587.2 6.6 collective-permute-start.16
  591.4 3.8 collective-permute-start.15
  610.0 8.1 %collective-permute-start.18 = (f32[4,4,4,128]{3,2,0,1:T(4,128)S(1)}, f32[4,4,4,128]{3,2,0,1:T(4,128)S(1)}, u32[]{:S(2)}, u32[]{:S(2)}) collective-permute-start(f32[4,4,4,128]{3,2,0,1:T(4,128)S(1)} %maximum_bitcast_fusion.57), channel_id=1, source_target_pairs={{1,0},{2,1},{3,2},{4,3},{5,4},{6,5},{7,6},{8,7},{9,8},{10,9},{11,1... | collective-permute-start | bytes 98312 | tf_op jit(solution)/shard_map/ppermute | solution.py:32
  615.4 2.7 collective-permute-start.17
  666.7 5.0 collective-permute-start.19
  (100 other events, 609.6 us)
where the time goes:
time: 732 us; the launch traced here: 719 us
  local copies, waits for them, and re-layouts  429 us (59%)
  other arithmetic  135 us (18%)
  blocking collectives  103 us (14%)
  starting transfers between devices  31 us (4%)
  between operations  10.7 us (1%)
  waiting for transfers between devices  8.46 us (1%)
    gather x17, local copies, waits for them, and re-layouts, coarse_fill(): window = jnp.take_along_axis(chosen, positions, axis=3)  175 us
    scatter x9, local copies, waits for them, and re-layouts, insert_blocks(): coarse = coarse.at[:3, :, row_start:row_start + quarter, col_start:col_st...  82.2 us
    pmax x2, blocking collectives, local(): fastest_all = lax.pmax(local_fast, 'patch')  59.3 us
    reshape x2, local copies, waits for them, and re-layouts, restrict_blocks(): part_state.reshape(3, patch_count, quarter, 4, quarter, 4).mean(axis=(3, 5))  56 us
    all_gather x2, blocking collectives, local(): strip_table = lax.all_gather(strips, 'patch', axis=0, tiled=True)  43.6 us
    unnamed x256, local copies, waits for them, and re-layouts  23.6 us
    slice x15, local copies, waits for them, and re-layouts, cycle_lines(): columns = [state[:, :, :, place] for place in line_pos]  20.6 us
    reduce_sum x2, other arithmetic, restrict_blocks(): part_state.reshape(3, patch_count, quarter, 4, quarter, 4).mean(axis=(3, 5))  19.5 us
  transfers between devices with their start and end apart: 20, of which 3 were waited for; matrix products, arithmetic and copies ran while one was open for 14% of the time, Pallas kernels for 0%

commit v1 on v0

v1 whole, which is shorter than its diff:
```python
import functools

import jax
import jax.numpy as jnp
from jax import lax
from jax.experimental import pallas as pl
from jax.experimental.pallas import tpu as pltpu
from jax.sharding import PartitionSpec as P

STEPS = 2
GRAVITY = 9.81
CFL_NUMBER = 0.3
GRID = 8
SIZE = 128
Q = SIZE // 4
STRIP = 32
COARSE = 4


def nt(a, b):
    return lax.dot_general(
        a, b, (((1,), (1,)), ((), ())), precision=lax.Precision.HIGHEST,
        preferred_element_type=jnp.float32,
    )


def derived(h, m, n):
    r = 1.0 / h
    u = m * r
    v = n * r
    c = jnp.sqrt(GRAVITY * h)
    p = (0.5 * GRAVITY) * (h * h)
    return (h, m, n, jnp.abs(u) + c, jnp.abs(v) + c, m * u + p, n * v + p, m * v)


def flux(left, right):
    a = jnp.maximum(left[3], right[3])
    return (
        (left[1] + right[1]) - a * (right[0] - left[0]),
        (left[4] + right[4]) - a * (right[1] - left[1]),
        (left[5] + right[5]) - a * (right[2] - left[2]),
    )


def along_x(d):
    return (d[0], d[1], d[2], d[3], d[5], d[7])


def along_y(d):
    return (d[0], d[2], d[1], d[4], d[6], d[7])


def speed_tile(h, m, n):
    s = jnp.maximum(jnp.abs(m), jnp.abs(n)) / h + jnp.sqrt(GRAVITY * h)
    return jnp.max(s.reshape(SIZE // 8, 8, SIZE), axis=0)


def kernel(
    devices,
    cd, cm, cb, fd, fm, fb, meta,
    cd_out, cm_out, fd_out, fm_out,
    prev_d, prev_m, prev_b, prev_meta, meta_s, side_s,
    state, bed, slope_x, slope_y, strips, strips_in, top, top_in, lines, wide, gcol, grow, back,
    local_sem, slot_send, slot_recv, edge_send, edge_recv, top_send, top_recv, back_send, back_recv,
):
    me = lax.axis_index("patch")
    nxt = lax.rem(me + 1, devices)
    before = lax.rem(me + devices - 1, devices)
    column = lax.rem(me, GRID)
    upper = lax.rem(me + (2 * GRID - 1) - 2 * column, devices)
    lower = lax.rem(me + devices - 1 - 2 * column, devices)
    partners = [before, nxt, upper, lower]
    opposite_slot = [1, 0, 3, 2]

    barrier = pltpu.get_barrier_semaphore()

    def greet(off, _):
        pl.semaphore_signal(
            barrier, inc=1, device_id={"patch": lax.rem(me + off, devices)},
            device_id_type=pl.DeviceIdType.MESH,
        )
        return 0

    lax.fori_loop(1, devices, greet, 0)

    lane = lax.broadcasted_iota(jnp.int32, (STRIP, SIZE), 1)
    row = lax.broadcasted_iota(jnp.int32, (STRIP, SIZE), 0)
    first_lane, last_lane = lane == 0, lane == SIZE - 1
    first_row, last_row = row == 0, row == STRIP - 1

    own_meta = pltpu.make_async_copy(meta, meta_s.at[1], local_sem.at[0])
    own_meta.start()

    er = lax.broadcasted_iota(jnp.int32, (8, SIZE), 0)
    ec = lax.broadcasted_iota(jnp.int32, (8, SIZE), 1)
    want = jnp.where(er == 0, 2 * Q, jnp.where(er == 1, Q - 1, jnp.where(er == 2, 3 * Q, jnp.where(
        er == 3, 2 * Q - 1, jnp.where(er == 4, 0, SIZE - 1)))))
    pick = (ec == want).astype(jnp.float32)
    ii = lax.broadcasted_iota(jnp.int32, (SIZE, SIZE), 0)
    jj = lax.broadcasted_iota(jnp.int32, (SIZE, SIZE), 1)
    eye = (ii == jj).astype(jnp.float32)
    offset = (lax.rem(ii, 4).astype(jnp.float32) - 1.5) * 0.25
    spread = [(jj == Q * (1 + r) + ii // 4).astype(jnp.float32) for r in range(2)]
    tilt = [s * offset for s in spread]
    gather_columns = [(ii == Q * (1 + r) + jj // 4).astype(jnp.float32) for r in range(2)]

    state[0, COARSE, 0] = cd[0]
    state[0, COARSE, 1] = cm[0, 0]
    state[0, COARSE, 2] = cm[1, 0]
    bed[COARSE] = cb[0]

    def coarse_field(which, f):
        return bed[COARSE] if f == 3 else state[which, COARSE, f]

    def take_lines(which):
        for f in range(4):
            value = coarse_field(which, f)
            found = nt(pick, value)
            for c in range(2):
                for side in range(2):
                    lines[0, which, pl.ds(c * 8 + f * 2 + side, 1), :] = found[c * 2 + side : c * 2 + side + 1]
            for c, (south, north) in enumerate(((Q - 1, 2 * Q), (2 * Q - 1, 3 * Q))):
                lines[1, which, pl.ds(c * 8 + f * 2, 1), :] = value[south : south + 1]
                lines[1, which, pl.ds(c * 8 + f * 2 + 1, 1), :] = value[north : north + 1]
            if which == 0:
                strips[pl.ds(f, 1), :] = found[4:5]
                strips[pl.ds(4 + f, 1), :] = found[5:6]
                strips[pl.ds(8 + f, 1), :] = value[0:1]
                strips[pl.ds(12 + f, 1), :] = value[SIZE - 1 : SIZE]

    def edge_copy(step, p):
        return pltpu.make_async_remote_copy(
            src_ref=strips,
            dst_ref=strips_in.at[step, opposite_slot[p]],
            send_sem=edge_send.at[step, p],
            recv_sem=edge_recv.at[step, opposite_slot[p]],
            device_id={"patch": partners[p]},
            device_id_type=pl.DeviceIdType.MESH,
        )

    def edge_arrival(step, p):
        return pltpu.make_async_remote_copy(
            src_ref=strips,
            dst_ref=strips_in.at[step, p],
            send_sem=edge_send.at[step, p],
            recv_sem=edge_recv.at[step, p],
            device_id={"patch": partners[p]},
            device_id_type=pl.DeviceIdType.MESH,
        )

    def top_copy(step, off):
        return pltpu.make_async_remote_copy(
            src_ref=top.at[step],
            dst_ref=top_in.at[step, off],
            send_sem=top_send.at[step, off],
            recv_sem=top_recv.at[step, off],
            device_id={"patch": lax.rem(me + off, devices)},
            device_id_type=pl.DeviceIdType.MESH,
        )

    own_meta.wait()
    fastest = speed_tile(cd[0], cm[0, 0], cm[1, 0])
    for j in range(4):
        tile = speed_tile(fd[j], fm[0, j], fm[1, j])
        fastest = jnp.maximum(fastest, jnp.where(meta_s[1, j, 0] > 0, tile, 0.0))
    top[0] = fastest
    take_lines(0)
    pl.semaphore_wait(barrier, devices - 1)

    def start_exchange(step):
        def send(off, _):
            top_copy(step, off).start()
            return 0

        lax.fori_loop(1, devices, send, 0)
        for p in range(4):
            edge_copy(step, p).start()

    start_exchange(0)
    to_next = {"patch": nxt}
    moves = [
        pltpu.make_async_remote_copy(
            src_ref=src, dst_ref=dst, send_sem=slot_send.at[i], recv_sem=slot_recv.at[i],
            device_id=to_next, device_id_type=pl.DeviceIdType.MESH,
        )
        for i, (src, dst) in enumerate(((meta, prev_meta), (fb, prev_b), (fd, prev_d), (fm, prev_m)))
    ]
    for move in moves:
        move.start()

    def ghost_column(old, f, shift):
        return pltpu.roll(old, shift, 1)

    def strip_bed(p, gci, lbase, gri, rbase):
        tile = grow[gri, pl.ds(pl.multiple_of(rbase, 8), 8), :]
        nb = [side_s[0, p * 4 + side] for side in range(4)]
        ok = [side_s[1, p * 4 + side] > 0 for side in range(4)]
        value = bed[p]
        big = lax.broadcasted_iota(jnp.int32, (SIZE, SIZE), 1)
        tall = lax.broadcasted_iota(jnp.int32, (SIZE, SIZE), 0)
        g = pltpu.roll(gcol[gci], lax.rem(2 * SIZE - (lbase + 7), SIZE), 1)
        west = jnp.where(ok[0], pltpu.roll(bed[nb[0]], 1, 1), g)
        east = jnp.where(ok[1], pltpu.roll(bed[nb[1]], SIZE - 1, 1), g)
        south = jnp.where(ok[2], bed[nb[2], SIZE - 1 : SIZE, :], tile[6:7])
        north = jnp.where(ok[3], bed[nb[3], 0:1, :], tile[7:8])
        bw = jnp.where(big == 0, west, pltpu.roll(value, 1, 1))
        be = jnp.where(big == SIZE - 1, east, pltpu.roll(value, SIZE - 1, 1))
        bs = jnp.where(tall == 0, south, pltpu.roll(value, 1, 0))
        bn = jnp.where(tall == SIZE - 1, north, pltpu.roll(value, SIZE - 1, 0))
        slope_x[p] = GRAVITY * (be - bw)
        slope_y[p] = GRAVITY * (bn - bs)

    def advance(p, src, gci, lbase, gri, rbase, half):
        dst = 1 - src
        tile = grow[gri, pl.ds(pl.multiple_of(rbase, 8), 8), :]
        nb = [side_s[0, p * 4 + side] for side in range(4)]
        ok = [side_s[1, p * 4 + side] > 0 for side in range(4)]
        live = side_s[2, p] > 0
        for i in range(SIZE // STRIP):
            r0 = i * STRIP
            rows = slice(r0, r0 + STRIP)
            cell = [state[src, p, f, rows, :] for f in range(3)]
            shared = gcol[gci, rows, :]
            ghost = []
            for f in range(3):
                g = pltpu.roll(shared, lax.rem(2 * SIZE - (lbase + f * 2 + 1), SIZE), 1)
                west = pltpu.roll(state[src, nb[0], f, rows, :], 1, 1)
                east = pltpu.roll(state[src, nb[1], f, rows, :], SIZE - 1, 1)
                ghost.append(
                    jnp.where(lane < SIZE // 2, jnp.where(ok[0], west, g), jnp.where(ok[1], east, g))
                )
            if i == 0:
                low = [
                    jnp.where(ok[2], state[src, nb[2], f, SIZE - 1 : SIZE, :], tile[f * 2 : f * 2 + 1])
                    for f in range(3)
                ]
            else:
                low = [state[src, p, f, r0 - 1 : r0, :] for f in range(3)]
            if i == SIZE // STRIP - 1:
                high = [
                    jnp.where(ok[3], state[src, nb[3], f, 0:1, :], tile[f * 2 + 1 : f * 2 + 2])
                    for f in range(3)
                ]
            else:
                high = [state[src, p, f, r0 + STRIP : r0 + STRIP + 1, :] for f in range(3)]
            here = derived(*cell)
            outside = along_x(derived(*ghost))
            hx = along_x(here)
            left = tuple(
                jnp.where(first_lane, o, pltpu.roll(x, 1, 1)) for o, x in zip(outside, hx)
            )
            fx = flux(left, hx)
            fe = flux(hx, outside)
            dx = [
                jnp.where(last_lane, e, pltpu.roll(w, SIZE - 1, 1)) - w for e, w in zip(fe, fx)
            ]
            hy = along_y(here)
            lowy = along_y(derived(*low))
            highy = along_y(derived(*high))
            below = tuple(
                jnp.where(first_row, o, pltpu.roll(y, 1, 0)) for o, y in zip(lowy, hy)
            )
            fy = flux(below, hy)
            fn = flux(tuple(y[STRIP - 1 : STRIP] for y in hy), highy)
            dy = [
                jnp.where(last_row, e, pltpu.roll(w, STRIP - 1, 0)) - w for e, w in zip(fn, fy)
            ]
            h = cell[0]
            new = (
                h - half * (dx[0] + dy[0]),
                cell[1] - half * (dx[1] + dy[2] + h * slope_x[p, rows, :]),
                cell[2] - half * (dx[2] + dy[1] + h * slope_y[p, rows, :]),
            )
            for f in range(3):
                state[dst, p, f, rows, :] = jnp.where(live, new[f], cell[f])

    for side in range(4):
        side_s[0, COARSE * 4 + side] = 0
        side_s[1, COARSE * 4 + side] = 0
    side_s[2, COARSE] = 1

    for step in range(STEPS):
        for p in range(4):
            edge_arrival(step, p).wait_recv()
        for side in range(4):
            n = meta_s[1, 4, side]
            other = slice(((1, 0, 3, 2)[side]) * 4, ((1, 0, 3, 2)[side]) * 4 + 4)
            found = strips_in[step, 3, other, :]
            for p in range(3):
                found = jnp.where(n == partners[p], strips_in[step, p, other, :], found)
            own = strips[side * 4 : side * 4 + 4, :]
            flip = lax.broadcasted_iota(jnp.int32, (4, SIZE), 0) == (1 if side < 2 else 2)
            values = jnp.where(n >= 0, found, jnp.where(flip, -own, own))
            for f in range(4):
                if side < 2:
                    wide[pl.ds(f * 2 + 1 - side, 1), :] = values[f : f + 1]
                else:
                    grow[2, pl.ds(f * 2 + side - 2, 1), :] = values[f : f + 1]
        gcol[2] = nt(eye, jnp.concatenate([wide[...]] * (SIZE // 8), axis=0))
        if step == 0:
            strip_bed(COARSE, 2, 0, 2, 0)

        def arrive(off, best):
            top_copy(step, off).wait_recv()
            return jnp.maximum(best, top_in[step, off])

        fastest = lax.fori_loop(1, devices, arrive, top[step])
        half = (0.5 * CFL_NUMBER) / jnp.max(fastest, keepdims=True)
        advance(COARSE, 0, 2, 0, 2, 0, half)
        take_lines(1)

        if step == 0:
            for move in moves:
                move.wait_recv()
            prev_copy = pltpu.make_async_copy(prev_meta, meta_s.at[0], local_sem.at[1])
            prev_copy.start()
            prev_copy.wait()
            kids = [meta_s[1, 5, b] for b in range(4)]
            for b in range(4):
                index = jnp.minimum(lax.rem(kids[b] - me * 4 + 4 + 4 * devices, 4 * devices), 7)
                near = index >= 4
                there = jnp.where(near, 0, index)
                here_at = jnp.where(near, index - 4, 0)
                which = near.astype(jnp.int32)
                slot = index - 4 * which
                side_s[2, b] = meta_s[which, slot, 0]
                for side in range(4):
                    n = meta_s[which, slot, 1 + side]
                    spot = jnp.where(n == kids[1], 1, jnp.where(n == kids[2], 2, jnp.where(n == kids[3], 3, 0)))
                    side_s[0, b * 4 + side] = spot
                    side_s[1, b * 4 + side] = jnp.where(n >= 0, 1, 0)
                    side_s[3, b * 4 + side] = meta_s[which, slot, 5 + side]
                state[0, b, 0] = jnp.where(near, fd[here_at], prev_d[there])
                state[0, b, 1] = jnp.where(near, fm[0, here_at], prev_m[0, there])
                state[0, b, 2] = jnp.where(near, fm[1, here_at], prev_m[1, there])
                bed[b] = jnp.where(near, fb[here_at], prev_b[there])

        rows64 = lax.broadcasted_iota(jnp.int32, (64, SIZE), 0)
        odd = lax.rem(rows64, 2) == 1
        second = lax.rem(rows64 // 8, 2) == 1
        for kind in range(2):
            parts = []
            for s in range(4):
                w = s / 4.0
                parts.append((1.0 - w) * lines[kind, 0] + w * lines[kind, 1])
            face = jnp.concatenate(parts, axis=0)
            rising = pltpu.roll(face, SIZE - 1, 1) - face
            falling = face - pltpu.roll(face, 1, 1)
            least = jnp.minimum(jnp.abs(rising), jnp.abs(falling))
            grad = jnp.where(rising * falling > 0, jnp.where(rising > 0, least, -least), 0.0)
            for r in range(2):
                if kind == 0:
                    m = [side_s[3, (2 * r + c) * 4 + side].astype(jnp.float32) for c in range(2) for side in (1, 0)]
                else:
                    m = [side_s[3, (2 * c + r) * 4 + side].astype(jnp.float32) for c in range(2) for side in (2, 3)]
                mode = jnp.where(second, jnp.where(odd, m[3], m[2]), jnp.where(odd, m[1], m[0]))
                leaning = grad * mode
                if kind == 0:
                    gcol[r] = nt(spread[r], jnp.concatenate([face, face], axis=0)) + nt(
                        tilt[r], jnp.concatenate([leaning, leaning], axis=0)
                    )
                else:
                    grow[r] = nt(face, spread[r]) + nt(leaning, tilt[r])
        if step == 0:
            for b in range(4):
                strip_bed(b, b // 2, (b % 2) * 8, b % 2, (b // 2) * 8)

        def substep(t, _):
            s, b = t // 4, lax.rem(t, 4)
            r, c = b // 2, lax.rem(b, 2)
            advance(b, lax.rem(s, 2), r, s * 16 + c * 8, c, s * 16 + r * 8, half)
            return 0

        lax.fori_loop(0, 16, substep, 0)

        if step == STEPS - 1:
            home = pltpu.make_async_remote_copy(
                src_ref=state.at[0, pl.ds(0, 4)], dst_ref=back, send_sem=back_send, recv_sem=back_recv,
                device_id={"patch": before}, device_id_type=pl.DeviceIdType.MESH,
            )
            home.start()

        small_lane = lax.broadcasted_iota(jnp.int32, (Q, SIZE), 1)
        for f in range(3):
            state[0, COARSE, f] = state[1, COARSE, f]
        for b in range(4):
            r, c = b // 2, b % 2
            sums = jnp.concatenate(
                [
                    functools.reduce(
                        jnp.add, [state[0, b, f, pl.ds(k, Q, stride=4), :] for k in range(4)]
                    )
                    for f in range(3)
                ],
                axis=0,
            )
            means = lax.dot_general(
                sums * (1.0 / 16.0), spread[c], (((1,), (0,)), ((), ())),
                precision=lax.Precision.HIGHEST, preferred_element_type=jnp.float32,
            )
            low_lane = Q * (1 + c)
            inside = (small_lane >= low_lane) & (small_lane < low_lane + Q)
            refined = meta_s[1, 6, b] > 0
            for f in range(3):
                held = state[0, COARSE, f, Q * (1 + r) : Q * (2 + r), :]
                fresh = jnp.where(refined, means[f * Q : f * Q + Q], held)
                state[0, COARSE, f, Q * (1 + r) : Q * (2 + r), :] = jnp.where(inside, fresh, held)

        for p in range(4):
            edge_arrival(step, p).wait_send()
        if step < STEPS - 1:
            fastest = speed_tile(state[0, COARSE, 0], state[0, COARSE, 1], state[0, COARSE, 2])
            for b in range(4):
                tile = speed_tile(state[0, b, 0], state[0, b, 1], state[0, b, 2])
                fastest = jnp.maximum(fastest, jnp.where(side_s[2, b] > 0, tile, 0.0))
            top[step + 1] = fastest
            take_lines(0)
            start_exchange(step + 1)

    cd_out[0] = state[0, COARSE, 0]
    cm_out[0, 0] = state[0, COARSE, 1]
    cm_out[1, 0] = state[0, COARSE, 2]
    for move in moves:
        move.wait_send()

    def sent(off, _):
        for step in range(STEPS):
            top_copy(step, off).wait_send()
        return 0

    lax.fori_loop(1, devices, sent, 0)
    home.wait()
    for j in range(4):
        mine = meta_s[1, j, 9] == me
        block = meta_s[1, j, 10]
        fd_out[j] = jnp.where(mine, state[0, block, 0], back[block, 0])
        fm_out[0, j] = jnp.where(mine, state[0, block, 1], back[block, 1])
        fm_out[1, j] = jnp.where(mine, state[0, block, 2], back[block, 2])


def local(
    coarse_depth, coarse_momentum, coarse_bed, fine_depth, fine_momentum, fine_bed,
    coarse_neighbors, coarse_children, coarse_refined, fine_parent, fine_block, fine_active,
    fine_neighbors, fill_mode,
):
    devices = lax.axis_size("patch")
    slots = jnp.concatenate(
        [fine_active[:, None], fine_neighbors, fill_mode, fine_parent[:, None], fine_block[:, None]], axis=1
    )
    family = jnp.concatenate([coarse_neighbors, coarse_children, coarse_refined], axis=0)
    meta = jnp.concatenate(
        [
            jnp.pad(slots, ((0, 0), (0, SIZE - slots.shape[1]))),
            jnp.pad(family, ((0, 1), (0, SIZE - family.shape[1]))),
        ],
        axis=0,
    )
    f32, i32 = jnp.float32, jnp.int32
    vmem = pl.BlockSpec(memory_space=pltpu.VMEM)
    dma = pltpu.SemaphoreType.DMA
    return tuple(
        pl.pallas_call(
            functools.partial(kernel, devices),
            out_shape=(
                jax.ShapeDtypeStruct(coarse_depth.shape, f32),
                jax.ShapeDtypeStruct(coarse_momentum.shape, f32),
                jax.ShapeDtypeStruct(fine_depth.shape, f32),
                jax.ShapeDtypeStruct(fine_momentum.shape, f32),
            ),
            in_specs=[vmem] * 7,
            out_specs=(vmem,) * 4,
            scratch_shapes=[
                pltpu.VMEM((4, SIZE, SIZE), f32),
                pltpu.VMEM((2, 4, SIZE, SIZE), f32),
                pltpu.VMEM((4, SIZE, SIZE), f32),
                pltpu.VMEM((8, SIZE), i32),
                pltpu.SMEM((2, 8, SIZE), i32),
                pltpu.SMEM((4, 20), i32),
                pltpu.VMEM((2, 5, 3, SIZE, SIZE), f32),
                pltpu.VMEM((5, SIZE, SIZE), f32),
                pltpu.VMEM((5, SIZE, SIZE), f32),
                pltpu.VMEM((5, SIZE, SIZE), f32),
                pltpu.VMEM((16, SIZE), f32),
                pltpu.VMEM((STEPS, 4, 16, SIZE), f32),
                pltpu.VMEM((STEPS, 8, SIZE), f32),
                pltpu.VMEM((STEPS, devices, 8, SIZE), f32),
                pltpu.VMEM((2, 2, 16, SIZE), f32),
                pltpu.VMEM((8, SIZE), f32),
                pltpu.VMEM((3, SIZE, SIZE), f32),
                pltpu.VMEM((3, 64, SIZE), f32),
                pltpu.VMEM((4, 3, SIZE, SIZE), f32),
                dma((2,)),
                dma((4,)),
                dma((4,)),
                dma((STEPS, 4)),
                dma((STEPS, 4)),
                dma((STEPS, devices)),
                dma((STEPS, devices)),
                dma(()),
                dma(()),
            ],
            compiler_params=pltpu.CompilerParams(
                collective_id=0, has_side_effects=True, vmem_limit_bytes=40 * 2**20
            ),
        )(coarse_depth, coarse_momentum, coarse_bed, fine_depth, fine_momentum, fine_bed, meta)
    )


def solution(mesh):
    lead = P(("groups", "patch"))
    second = P(None, ("groups", "patch"))
    return jax.shard_map(
        local,
        mesh=mesh,
        in_specs=(lead, second, lead, lead, second, lead) + (lead,) * 8,
        out_specs=(lead, second, lead, second),
        check_vma=False,
    )
```

time: 732 us -> 81.1 us (0.11); the launches traced: 719 us -> 80.7 us
  local copies, waits for them, and re-layouts: 429 us -> 11.1 us
  other arithmetic: 135 us -> 0.02 us
  blocking collectives: 103 us -> 0 us
  Pallas kernels: 0 us -> 69 us
  starting transfers between devices: 31 us -> 0 us
  between operations: 10.7 us -> 0.69 us
  waiting for transfers between devices: 8.46 us -> 0 us
    gather x31 -> x0, local copies, waits for them, and re-layouts: 184 us -> none  [the longest x17 175 us: coarse_fill(): window = jnp.take_along_axis(chosen, positions, axis=3)]
    scatter x9 -> x0, local copies, waits for them, and re-layouts: 82.2 us -> none  [insert_blocks(): coarse = coarse.at[:3, :, row_start:row_start + quarter, col_start:col_st...]
    reshape x22 -> x0, local copies, waits for them, and re-layouts: 70.4 us -> none  [the longest x2 56 us: restrict_blocks(): part_state.reshape(3, patch_count, quarter, 4, quarter, 4).mean(axis=(3, 5))]
    pallas_call x0 -> x1, Pallas kernels: none -> 69 us  [local(): pl.pallas_call(functools.partial(kernel, devices), out_shape=(jax.ShapeDt...]
    pmax x2 -> x0, blocking collectives: 59.3 us -> none  [local(): fastest_all = lax.pmax(local_fast, 'patch')]
    all_gather x2 -> x0, blocking collectives: 43.6 us -> none  [local(): strip_table = lax.all_gather(strips, 'patch', axis=0, tiled=True)]
    slice x47 -> x0, local copies, waits for them, and re-layouts: 35.5 us -> none  [the longest x15 20.6 us: cycle_lines(): columns = [state[:, :, :, place] for place in line_pos]]
    ppermute x20 -> x0, starting transfers between devices: 31 us -> none  [the longest x8 18.2 us: padded_2(): after = lax.ppermute(initial, axis, down)]
  transfers between devices with their start and end apart: 20 -> 0, of which waited for: 3 -> 0; matrix products, arithmetic and copies ran while one was open for 14% -> 0% of each run, Pallas kernels for 0% -> 0%
where the time goes in v1:
time: 81.1 us; the launch traced here: 80.7 us
  Pallas kernels  69 us (85%)
  local copies, waits for them, and re-layouts  11.1 us (14%)
    pallas_call x1, Pallas kernels, local(): pl.pallas_call(functools.partial(kernel, devices), out_shape=(jax.ShapeDt...  69 us
    unnamed x32, local copies, waits for them, and re-layouts  10.7 us

profile of v1, /device:TPU:1, one launch (start us, length us, event | category | flops | bytes accessed | tf_op | source)
XLA Modules:
  0.0 80.7 jit_solution(10043863195319700269)
XLA Ops:
  0.6 0.0 copy-start.8
  0.6 0.0 copy-start.9
  0.7 0.6 copy-done.8
  1.3 0.0 copy-done.9
  1.3 0.0 copy-done.10
  1.3 0.6 copy-done.11
  2.0 0.1 copy.19
  2.1 0.6 copy-done.12
  2.6 0.1 copy.20
  2.7 0.1 copy.18
  2.8 0.5 copy-done.6
  3.3 0.0 copy-done.7
  3.3 0.1 concatenate.9
  3.4 1.0 %copy-done = f32[2,4,128,128]{3,2,1,0:T(8,128)S(1)} copy-done((f32[2,4,128,128]{3,2,1,0:T(8,128)S(1)}, f32[2,4,128,128]{3,2,1,0:T(8,128)}, u32[]{:S(2)}) %copy-start) | copy-done | bytes 524312
  4.5 0.9 %copy-done.1 = f32[4,128,128]{2,1,0:T(8,128)S(1)} copy-done((f32[4,128,128]{2,1,0:T(8,128)S(1)}, f32[4,128,128]{2,1,0:T(8,128)}, u32[]{:S(2)}) %copy-start.1) | copy-done | bytes 262168
  5.4 0.9 %copy-done.2 = f32[4,128,128]{2,1,0:T(8,128)S(1)} copy-done((f32[4,128,128]{2,1,0:T(8,128)S(1)}, f32[4,128,128]{2,1,0:T(8,128)}, u32[]{:S(2)}) %copy-start.2) | copy-done | bytes 262168
  6.4 0.9 %copy-done.3 = f32[2,1,128,128]{3,2,1,0:T(8,128)S(1)} copy-done((f32[2,1,128,128]{3,2,1,0:T(8,128)S(1)}, f32[2,1,128,128]{3,2,1,0:T(8,128)}, u32[]{:S(2)}) %copy-start.3) | copy-done | bytes 131096
  7.3 0.8 %copy-done.4 = f32[1,128,128]{2,1,0:T(8,128)S(1)} copy-done((f32[1,128,128]{2,1,0:T(8,128)S(1)}, f32[1,128,128]{2,1,0:T(8,128)}, u32[]{:S(2)}) %copy-start.4) | copy-done | bytes 65560
  8.1 0.8 %copy-done.5 = f32[1,128,128]{2,1,0:T(8,128)S(1)} copy-done((f32[1,128,128]{2,1,0:T(8,128)S(1)}, f32[1,128,128]{2,1,0:T(8,128)}, u32[]{:S(2)}) %copy-start.5) | copy-done | bytes 65560
  9.0 69.0 %shard_map.165 = (f32[1,128,128]{2,1,0:T(8,128)S(1)}, f32[2,1,128,128]{3,2,1,0:T(8,128)S(1)}, f32[4,128,128]{2,1,0:T(8,128)S(1)}, f32[2,4,128,128]{3,2,1,0:T(8,128)S(1)}) custom-call(f32[1,128,128]{2,1,0:T(8,128)S(1)} %copy-done.4, f32[2,1,128,128]{3,2,1,0:T(8,128)S(1)} %copy-done.3, f32[1,128,128]{2,1,0:T(8,128)S(1)} %copy-done.5, ...), custom_call_target="tpu_custom_call" | custom-call | tf_op jit(solution)/shard_map/pallas_call | solution.py:462
  77.9 0.6 copy.25
  78.6 0.7 copy.26
  79.2 0.7 copy.27
  79.9 0.8 copy.28
  (15 shorter events, 0.0 us)
Async XLA Ops:
  0.6 0.7 copy-start.8
  0.6 0.7 copy-start.9
  0.7 0.7 copy-start.10
  1.3 0.7 copy-start.11
  2.0 0.7 copy-start.12
  2.0 0.8 copy-start.13
  2.6 0.7 copy-start.6
  2.6 0.7 copy-start.7
  3.4 1.0 %copy-start = (f32[2,4,128,128]{3,2,1,0:T(8,128)S(1)}, f32[2,4,128,128]{3,2,1,0:T(8,128)}, u32[]{:S(2)}) copy-start(f32[2,4,128,128]{3,2,1,0:T(8,128)} %fm.1) | copy-start | bytes 1572868
  4.5 0.9 %copy-start.1 = (f32[4,128,128]{2,1,0:T(8,128)S(1)}, f32[4,128,128]{2,1,0:T(8,128)}, u32[]{:S(2)}) copy-start(f32[4,128,128]{2,1,0:T(8,128)} %fd.1) | copy-start | bytes 786436
  5.4 0.9 %copy-start.2 = (f32[4,128,128]{2,1,0:T(8,128)S(1)}, f32[4,128,128]{2,1,0:T(8,128)}, u32[]{:S(2)}) copy-start(f32[4,128,128]{2,1,0:T(8,128)} %fb.1) | copy-start | bytes 786436
  6.4 0.9 %copy-start.3 = (f32[2,1,128,128]{3,2,1,0:T(8,128)S(1)}, f32[2,1,128,128]{3,2,1,0:T(8,128)}, u32[]{:S(2)}) copy-start(f32[2,1,128,128]{3,2,1,0:T(8,128)} %cm.1) | copy-start | bytes 393220
  7.3 0.8 %copy-start.4 = (f32[1,128,128]{2,1,0:T(8,128)S(1)}, f32[1,128,128]{2,1,0:T(8,128)}, u32[]{:S(2)}) copy-start(f32[1,128,128]{2,1,0:T(8,128)} %cd.1) | copy-start | bytes 196612
  8.1 0.8 %copy-start.5 = (f32[1,128,128]{2,1,0:T(8,128)S(1)}, f32[1,128,128]{2,1,0:T(8,128)}, u32[]{:S(2)}) copy-start(f32[1,128,128]{2,1,0:T(8,128)} %cb.1) | copy-start | bytes 196612

commit v2 on v1

--- a/solution.py
+++ b/solution.py
@@ -57,11 +57,13 @@
 
 def kernel(
     devices,
-    cd, cm, cb, fd, fm, fb, meta,
+    cd_in, cm_in, cb_in, fd_in, fm_in, fb_in,
+    around_in, kids_in, refined_in, parent_in, block_in, active_in, beside_in, mode_in,
     cd_out, cm_out, fd_out, fm_out,
-    prev_d, prev_m, prev_b, prev_meta, meta_s, side_s,
+    fd, fm, fb, around_s, kids_s, refined_s, parent_s, block_s, active_s, beside_s, mode_s,
+    prev_d, prev_m, prev_b, prev_beside, prev_mode, side_s,
     state, bed, slope_x, slope_y, strips, strips_in, top, top_in, lines, wide, gcol, grow, back,
-    local_sem, slot_send, slot_recv, edge_send, edge_recv, top_send, top_recv, back_send, back_recv,
+    load_sem, local_sem, slot_send, slot_recv, edge_send, edge_recv, top_send, top_recv, back_send, back_recv,
 ):
     me = lax.axis_index("patch")
     nxt = lax.rem(me + 1, devices)
@@ -88,8 +90,18 @@
     first_lane, last_lane = lane == 0, lane == SIZE - 1
     first_row, last_row = row == 0, row == STRIP - 1
 
-    own_meta = pltpu.make_async_copy(meta, meta_s.at[1], local_sem.at[0])
-    own_meta.start()
+    loads = [
+        pltpu.make_async_copy(src, dst, load_sem.at[i])
+        for i, (src, dst) in enumerate((
+            (active_in, active_s), (fd_in, fd), (fm_in, fm),
+            (cd_in.at[0], state.at[0, COARSE, 0]), (cm_in.at[0, 0], state.at[0, COARSE, 1]),
+            (cm_in.at[1, 0], state.at[0, COARSE, 2]), (cb_in.at[0], bed.at[COARSE]), (fb_in, fb),
+            (around_in, around_s), (kids_in, kids_s), (refined_in, refined_s), (parent_in, parent_s),
+            (block_in, block_s), (beside_in, beside_s.at[1]), (mode_in, mode_s.at[1]),
+        ))
+    ]
+    for load in loads:
+        load.start()
 
     er = lax.broadcasted_iota(jnp.int32, (8, SIZE), 0)
     ec = lax.broadcasted_iota(jnp.int32, (8, SIZE), 1)
@@ -103,11 +115,6 @@
     spread = [(jj == Q * (1 + r) + ii // 4).astype(jnp.float32) for r in range(2)]
     tilt = [s * offset for s in spread]
     gather_columns = [(ii == Q * (1 + r) + jj // 4).astype(jnp.float32) for r in range(2)]
-
-    state[0, COARSE, 0] = cd[0]
-    state[0, COARSE, 1] = cm[0, 0]
-    state[0, COARSE, 2] = cm[1, 0]
-    bed[COARSE] = cb[0]
 
     def coarse_field(which, f):
         return bed[COARSE] if f == 3 else state[which, COARSE, f]
@@ -158,11 +165,12 @@
             device_id_type=pl.DeviceIdType.MESH,
         )
 
-    own_meta.wait()
-    fastest = speed_tile(cd[0], cm[0, 0], cm[1, 0])
+    for load in loads:
+        load.wait()
+    fastest = speed_tile(state[0, COARSE, 0], state[0, COARSE, 1], state[0, COARSE, 2])
     for j in range(4):
         tile = speed_tile(fd[j], fm[0, j], fm[1, j])
-        fastest = jnp.maximum(fastest, jnp.where(meta_s[1, j, 0] > 0, tile, 0.0))
+        fastest = jnp.maximum(fastest, jnp.where(active_s[j] > 0, tile, 0.0))
     top[0] = fastest
     take_lines(0)
     pl.semaphore_wait(barrier, devices - 1)
@@ -183,7 +191,9 @@
             src_ref=src, dst_ref=dst, send_sem=slot_send.at[i], recv_sem=slot_recv.at[i],
             device_id=to_next, device_id_type=pl.DeviceIdType.MESH,
         )
-        for i, (src, dst) in enumerate(((meta, prev_meta), (fb, prev_b), (fd, prev_d), (fm, prev_m)))
+        for i, (src, dst) in enumerate((
+            (beside_in, prev_beside), (mode_in, prev_mode), (fb, prev_b), (fd, prev_d), (fm, prev_m)
+        ))
     ]
     for move in moves:
         move.start()
@@ -283,7 +293,7 @@
         for p in range(4):
             edge_arrival(step, p).wait_recv()
         for side in range(4):
-            n = meta_s[1, 4, side]
+            n = around_s[0, side]
             other = slice(((1, 0, 3, 2)[side]) * 4, ((1, 0, 3, 2)[side]) * 4 + 4)
             found = strips_in[step, 3, other, :]
             for p in range(3):
@@ -312,10 +322,15 @@
         if step == 0:
             for move in moves:
                 move.wait_recv()
-            prev_copy = pltpu.make_async_copy(prev_meta, meta_s.at[0], local_sem.at[1])
-            prev_copy.start()
-            prev_copy.wait()
-            kids = [meta_s[1, 5, b] for b in range(4)]
+            ints = [
+                pltpu.make_async_copy(prev_beside, beside_s.at[0], local_sem.at[0]),
+                pltpu.make_async_copy(prev_mode, mode_s.at[0], local_sem.at[1]),
+            ]
+            for copy in ints:
+                copy.start()
+            for copy in ints:
+                copy.wait()
+            kids = [kids_s[0, b] for b in range(4)]
             for b in range(4):
                 index = jnp.minimum(lax.rem(kids[b] - me * 4 + 4 + 4 * devices, 4 * devices), 7)
                 near = index >= 4
@@ -323,13 +338,13 @@
                 here_at = jnp.where(near, index - 4, 0)
                 which = near.astype(jnp.int32)
                 slot = index - 4 * which
-                side_s[2, b] = meta_s[which, slot, 0]
+                side_s[2, b] = refined_s[0, b]
                 for side in range(4):
-                    n = meta_s[which, slot, 1 + side]
+                    n = beside_s[which, slot, side]
                     spot = jnp.where(n == kids[1], 1, jnp.where(n == kids[2], 2, jnp.where(n == kids[3], 3, 0)))
                     side_s[0, b * 4 + side] = spot
                     side_s[1, b * 4 + side] = jnp.where(n >= 0, 1, 0)
-                    side_s[3, b * 4 + side] = meta_s[which, slot, 5 + side]
+                    side_s[3, b * 4 + side] = mode_s[which, slot, side]
                 state[0, b, 0] = jnp.where(near, fd[here_at], prev_d[there])
                 state[0, b, 1] = jnp.where(near, fm[0, here_at], prev_m[0, there])
                 state[0, b, 2] = jnp.where(near, fm[1, here_at], prev_m[1, there])
@@ -400,7 +415,7 @@
             )
             low_lane = Q * (1 + c)
             inside = (small_lane >= low_lane) & (small_lane < low_lane + Q)
-            refined = meta_s[1, 6, b] > 0
+            refined = refined_s[0, b] > 0
             for f in range(3):
                 held = state[0, COARSE, f, Q * (1 + r) : Q * (2 + r), :]
                 fresh = jnp.where(refined, means[f * Q : f * Q + Q], held)
@@ -431,8 +446,8 @@
     lax.fori_loop(1, devices, sent, 0)
     home.wait()
     for j in range(4):
-        mine = meta_s[1, j, 9] == me
-        block = meta_s[1, j, 10]
+        mine = parent_s[j] == me
+        block = block_s[j]
         fd_out[j] = jnp.where(mine, state[0, block, 0], back[block, 0])
         fm_out[0, j] = jnp.where(mine, state[0, block, 1], back[block, 1])
         fm_out[1, j] = jnp.where(mine, state[0, block, 2], back[block, 2])
@@ -444,17 +459,6 @@
     fine_neighbors, fill_mode,
 ):
     devices = lax.axis_size("patch")
-    slots = jnp.concatenate(
-        [fine_active[:, None], fine_neighbors, fill_mode, fine_parent[:, None], fine_block[:, None]], axis=1
-    )
-    family = jnp.concatenate([coarse_neighbors, coarse_children, coarse_refined], axis=0)
-    meta = jnp.concatenate(
-        [
-            jnp.pad(slots, ((0, 0), (0, SIZE - slots.shape[1]))),
-            jnp.pad(family, ((0, 1), (0, SIZE - family.shape[1]))),
-        ],
-        axis=0,
-    )
     f32, i32 = jnp.float32, jnp.int32
     vmem = pl.BlockSpec(memory_space=pltpu.VMEM)
     dma = pltpu.SemaphoreType.DMA
@@ -467,14 +471,25 @@
                 jax.ShapeDtypeStruct(fine_depth.shape, f32),
                 jax.ShapeDtypeStruct(fine_momentum.shape, f32),
             ),
-            in_specs=[vmem] * 7,
+            in_specs=[pl.BlockSpec(memory_space=pl.ANY)] * 14,
             out_specs=(vmem,) * 4,
             scratch_shapes=[
                 pltpu.VMEM((4, SIZE, SIZE), f32),
                 pltpu.VMEM((2, 4, SIZE, SIZE), f32),
                 pltpu.VMEM((4, SIZE, SIZE), f32),
-                pltpu.VMEM((8, SIZE), i32),
-                pltpu.SMEM((2, 8, SIZE), i32),
+                pltpu.SMEM((1, 4), i32),
+                pltpu.SMEM((1, 4), i32),
+                pltpu.SMEM((1, 4), i32),
+                pltpu.SMEM((4,), i32),
+                pltpu.SMEM((4,), i32),
+                pltpu.SMEM((4,), i32),
+                pltpu.SMEM((2, 4, 4), i32),
+                pltpu.SMEM((2, 4, 4), i32),
+                pltpu.VMEM((4, SIZE, SIZE), f32),
+                pltpu.VMEM((2, 4, SIZE, SIZE), f32),
+                pltpu.VMEM((4, SIZE, SIZE), f32),
+                pltpu.VMEM((4, 4), i32),
+                pltpu.VMEM((4, 4), i32),
                 pltpu.SMEM((4, 20), i32),
                 pltpu.VMEM((2, 5, 3, SIZE, SIZE), f32),
                 pltpu.VMEM((5, SIZE, SIZE), f32),
@@ -489,9 +504,10 @@
                 pltpu.VMEM((3, SIZE, SIZE), f32),
                 pltpu.VMEM((3, 64, SIZE), f32),
                 pltpu.VMEM((4, 3, SIZE, SIZE), f32),
+                dma((15,)),
                 dma((2,)),
-                dma((4,)),
-                dma((4,)),
+                dma((5,)),
+                dma((5,)),
                 dma((STEPS, 4)),
                 dma((STEPS, 4)),
                 dma((STEPS, devices)),
@@ -500,9 +516,11 @@
                 dma(()),
             ],
             compiler_params=pltpu.CompilerParams(
-                collective_id=0, has_side_effects=True, vmem_limit_bytes=40 * 2**20
+                collective_id=0, has_side_effects=True, vmem_limit_bytes=56 * 2**20
             ),
-        )(coarse_depth, coarse_momentum, coarse_bed, fine_depth, fine_momentum, fine_bed, meta)
+        )(coarse_depth, coarse_momentum, coarse_bed, fine_depth, fine_momentum, fine_bed,
+          coarse_neighbors, coarse_children, coarse_refined, fine_parent, fine_block, fine_active,
+          fine_neighbors, fill_mode)
     )
 
 

time: 81.1 us -> 76.5 us (0.943)
  local copies, waits for them, and re-layouts: 11.1 us -> 5.56 us
  Pallas kernels: 69 us -> 70.1 us
    unnamed x32 -> x6, local copies, waits for them, and re-layouts: 10.7 us -> 5.56 us
    pallas_call x1, Pallas kernels: 69 us -> 70.1 us  [local(): pl.pallas_call(functools.partial(kernel, devices), out_shape=(jax.ShapeDt...]
where the time goes in v2:
time: 76.5 us; the launch traced here: 76.3 us
  Pallas kernels  70.1 us (92%)
  local copies, waits for them, and re-layouts  5.56 us (7%)
    pallas_call x1, Pallas kernels, local(): pl.pallas_call(functools.partial(kernel, devices), out_shape=(jax.ShapeDt...  70.1 us
    unnamed x6, local copies, waits for them, and re-layouts  5.56 us

profile of v2, /device:TPU:1, one launch (start us, length us, event | category | flops | bytes accessed | tf_op | source)
XLA Modules:
  0.0 76.3 jit_solution(14425541572729628909)
XLA Ops:
  0.6 70.1 %shard_map.165 = (f32[1,128,128]{2,1,0:T(8,128)}, f32[2,1,128,128]{3,2,1,0:T(8,128)}, f32[4,128,128]{2,1,0:T(8,128)}, f32[2,4,128,128]{3,2,1,0:T(8,128)}) custom-call(f32[1,128,128]{2,1,0:T(8,128)} %cd_in.1, f32[2,1,128,128]{3,2,1,0:T(8,128)} %cm_in.1, f32[1,128,128]{2,1,0:T(8,128)} %cb_in.1, f32[4,128,128]{2,1,0:T(8,128)} %fd_in.1, ...), custom_call_target="tpu_custom_call" | custom-call | tf_op jit(solution)/shard_map/pallas_call | solution.py:466
  70.7 0.0 copy-start
  70.8 1.5 %copy.22 = f32[1,128,128]{2,1,0:T(8,128)} copy(f32[1,128,128]{2,1,0:T(8,128)} %get-tuple-element.8) | data formatting | bytes 131072
  72.3 1.6 %copy.23 = f32[2,1,128,128]{3,2,1,0:T(8,128)} copy(f32[2,1,128,128]{3,2,1,0:T(8,128)} %get-tuple-element.9) | data formatting | bytes 262144
  73.9 1.7 %copy.24 = f32[4,128,128]{2,1,0:T(8,128)} copy(f32[4,128,128]{2,1,0:T(8,128)} %get-tuple-element.10) | data formatting | bytes 524288
  75.5 0.0 copy-done
  75.5 0.8 %copy.25 = f32[2,4,128,128]{3,2,1,0:T(8,128)} copy(f32[2,4,128,128]{3,2,1,0:T(8,128)S(1)} %copy-done) | data formatting | bytes 1048576
Async XLA Ops:
  70.7 4.8 %copy-start = (f32[2,4,128,128]{3,2,1,0:T(8,128)S(1)}, f32[2,4,128,128]{3,2,1,0:T(8,128)}, u32[]{:S(2)}) copy-start(f32[2,4,128,128]{3,2,1,0:T(8,128)} %get-tuple-element.11) | copy-start | bytes 1572868

commit v3 on v2

--- a/solution.py
+++ b/solution.py
@@ -13,7 +13,7 @@
 GRID = 8
 SIZE = 128
 Q = SIZE // 4
-STRIP = 32
+STRIP = 128
 COARSE = 4
 
 
@@ -284,6 +284,12 @@
             for f in range(3):
                 state[dst, p, f, rows, :] = jnp.where(live, new[f], cell[f])
 
+    def home_copy(b):
+        return pltpu.make_async_remote_copy(
+            src_ref=state.at[0, b], dst_ref=back.at[b], send_sem=back_send.at[b], recv_sem=back_recv.at[b],
+            device_id={"patch": before}, device_id_type=pl.DeviceIdType.MESH,
+        )
+
     for side in range(4):
         side_s[0, COARSE * 4 + side] = 0
         side_s[1, COARSE * 4 + side] = 0
@@ -386,14 +392,17 @@
             advance(b, lax.rem(s, 2), r, s * 16 + c * 8, c, s * 16 + r * 8, half)
             return 0
 
-        lax.fori_loop(0, 16, substep, 0)
-
-        if step == STEPS - 1:
-            home = pltpu.make_async_remote_copy(
-                src_ref=state.at[0, pl.ds(0, 4)], dst_ref=back, send_sem=back_send, recv_sem=back_recv,
-                device_id={"patch": before}, device_id_type=pl.DeviceIdType.MESH,
-            )
-            home.start()
+        if step < STEPS - 1:
+            lax.fori_loop(0, 16, substep, 0)
+        else:
+            lax.fori_loop(0, 12, substep, 0)
+
+            def last(b, _):
+                substep(12 + b, 0)
+                home_copy(b).start()
+                return 0
+
+            lax.fori_loop(0, 4, last, 0)
 
         small_lane = lax.broadcasted_iota(jnp.int32, (Q, SIZE), 1)
         for f in range(3):
@@ -444,7 +453,8 @@
         return 0
 
     lax.fori_loop(1, devices, sent, 0)
-    home.wait()
+    for b in range(4):
+        home_copy(b).wait()
     for j in range(4):
         mine = parent_s[j] == me
         block = block_s[j]
@@ -512,8 +522,8 @@
                 dma((STEPS, 4)),
                 dma((STEPS, devices)),
                 dma((STEPS, devices)),
-                dma(()),
-                dma(()),
+                dma((4,)),
+                dma((4,)),
             ],
             compiler_params=pltpu.CompilerParams(
                 collective_id=0, has_side_effects=True, vmem_limit_bytes=56 * 2**20

time: 76.5 us -> 65.9 us (0.86)
  Pallas kernels: 70.1 us -> 59.5 us
    pallas_call x1, Pallas kernels: 70.1 us -> 59.5 us  [local(): pl.pallas_call(functools.partial(kernel, devices), out_shape=(jax.ShapeDt...]
where the time goes in v3:
time: 65.9 us; the launch traced here: 65.7 us
  Pallas kernels  59.5 us (90%)
  local copies, waits for them, and re-layouts  5.56 us (8%)
    pallas_call x1, Pallas kernels, local(): pl.pallas_call(functools.partial(kernel, devices), out_shape=(jax.ShapeDt...  59.5 us
    unnamed x6, local copies, waits for them, and re-layouts  5.56 us

profile of v3, /device:TPU:1, one launch (start us, length us, event | category | flops | bytes accessed | tf_op | source)
XLA Modules:
  0.0 65.7 jit_solution(10441186187803334461)
XLA Ops:
  0.6 59.5 %shard_map.165 = (f32[1,128,128]{2,1,0:T(8,128)}, f32[2,1,128,128]{3,2,1,0:T(8,128)}, f32[4,128,128]{2,1,0:T(8,128)}, f32[2,4,128,128]{3,2,1,0:T(8,128)}) custom-call(f32[1,128,128]{2,1,0:T(8,128)} %cd_in.1, f32[2,1,128,128]{3,2,1,0:T(8,128)} %cm_in.1, f32[1,128,128]{2,1,0:T(8,128)} %cb_in.1, f32[4,128,128]{2,1,0:T(8,128)} %fd_in.1, ...), custom_call_target="tpu_custom_call" | custom-call | tf_op jit(solution)/shard_map/pallas_call | solution.py:476
  60.2 0.0 copy-start
  60.2 1.5 %copy.22 = f32[1,128,128]{2,1,0:T(8,128)} copy(f32[1,128,128]{2,1,0:T(8,128)} %get-tuple-element.8) | data formatting | bytes 131072
  61.7 1.6 %copy.23 = f32[2,1,128,128]{3,2,1,0:T(8,128)} copy(f32[2,1,128,128]{3,2,1,0:T(8,128)} %get-tuple-element.9) | data formatting | bytes 262144
  63.3 1.7 %copy.24 = f32[4,128,128]{2,1,0:T(8,128)} copy(f32[4,128,128]{2,1,0:T(8,128)} %get-tuple-element.10) | data formatting | bytes 524288
  64.9 0.0 copy-done
  64.9 0.8 %copy.25 = f32[2,4,128,128]{3,2,1,0:T(8,128)} copy(f32[2,4,128,128]{3,2,1,0:T(8,128)S(1)} %copy-done) | data formatting | bytes 1048576
Async XLA Ops:
  60.2 4.8 %copy-start = (f32[2,4,128,128]{3,2,1,0:T(8,128)S(1)}, f32[2,4,128,128]{3,2,1,0:T(8,128)}, u32[]{:S(2)}) copy-start(f32[2,4,128,128]{3,2,1,0:T(8,128)} %get-tuple-element.11) | copy-start | bytes 1572868
